TPU v7x, 128 devices: a whole 4x4x4 slice. The times are simulated.
128 devices in a mesh: expert: 8 (over z_lo, y), dp: 16 (over z_hi, x, core).
Axes of the slice: x: 4, y: 4, z: 4 (z_hi: 2, z_lo: 2; z = z_hi * 2 + z_lo), core: 2. Of those that a mesh axis runs over, the one named last changes fastest.
Arguments:
- tokens: bfloat16 [2048, 7168], P('dp', 'expert'), may hold values from -6 to 6
- grad_out: bfloat16 [2048, 7168], P('dp', 'expert'), may hold values from -6 to 6
- expert_ids: int32 [2048, 2], P('dp'), may hold values from -1 to 7, as said below
- route_weights: float32 [2048, 2], P('dp'), may hold values from 0.1 to 1
- w_gate: bfloat16 [8, 7168, 2048], P('expert', 'dp'), may hold values from -0.0625 to 0.0625
- w_up: bfloat16 [8, 7168, 2048], P('expert', 'dp'), may hold values from -0.0625 to 0.0625
- w_down: bfloat16 [8, 2048, 7168], P('expert', None, 'dp'), may hold values from -0.125 to 0.125
Outputs:
- grad_tokens: bfloat16 [2048, 7168], P('dp', 'expert')
- grad_gate: bfloat16 [8, 7168, 2048], P('expert', 'dp')
- grad_up: bfloat16 [8, 7168, 2048], P('expert', 'dp')
- grad_down: bfloat16 [8, 2048, 7168], P('expert', None, 'dp')
Inputs may be any that keep to these rules, and one draw needn't show every extreme that they name: expert_ids[t, 0] is an expert; expert_ids[t, 1] is another expert or -1. Within each block of 128 rows (the tokens of one index of dp) no expert appears in more than 64 rows, and one expert, the same in every block, appears in exactly 64 rows, each of which has -1 as its second entry.
All inputs are finite; a program needn't handle non-finite values.
Results may differ from a plain program's by a relative error of at most 0.03.
Values may be sent and summed in bfloat16 or wider, within the bound.
A program may use at most 128 MiB of HBM per device.

v0:
```python
import math
import jax
import jax.numpy as jnp
from jax import lax
from jax.sharding import PartitionSpec as P


def body(tokens, grad_out, expert_ids, route_weights, w_gate, w_up, w_down):
    experts = lax.axis_size("expert")
    groups = lax.axis_size("dp")
    tok_rows, width = tokens.shape
    capacity = tok_rows // 2
    hidden = w_gate.shape[2]
    slots = groups * capacity
    expert_index = lax.axis_index("expert")
    inv_root = 1.0 / math.sqrt(tok_rows * groups)
    rows_first = (((0,), (0,)), ((), ()))
    last_dims = (((1,), (1,)), ((), ()))
    gate_shard, up_shard, down_shard = (w_gate[0], w_up[0], w_down[0])
    shard = gate_shard.shape[0]
    halves = width // shard
    names = jnp.arange(experts, dtype=jnp.int32)[:, None]
    hit0 = expert_ids[:, 0][None, :] == names
    hit1 = expert_ids[:, 1][None, :] == names
    hit = (hit0 | hit1).astype(jnp.bfloat16)
    index = jnp.arange(tok_rows, dtype=jnp.int32)
    before = (index[:, None] < index[None, :]).astype(jnp.bfloat16)
    rank = jnp.dot(hit, before, preferred_element_type=jnp.float32)
    rank = jnp.where(hit > 0, rank, -1.0).astype(jnp.int32)
    chosen = rank[:, None, :] == jnp.arange(capacity, dtype=jnp.int32)[None, :, None]
    dispatch = chosen.astype(jnp.bfloat16).reshape(experts * capacity, tok_rows)
    weight_of = jnp.where(hit0, route_weights[:, 0][None, :], 0.0) + jnp.where(
        hit1, route_weights[:, 1][None, :], 0.0
    )
    own_rank = lax.dynamic_slice_in_dim(rank, expert_index, 1)
    own_weight_of = lax.dynamic_slice_in_dim(weight_of, expert_index, 1)
    own_weight = jnp.sum(
        jnp.where(own_rank == jnp.arange(capacity, dtype=jnp.int32)[:, None], own_weight_of, 0.0),
        axis=1,
    )

    def send(rows):
        picked = [
            jnp.dot(
                dispatch, rows[:, h * shard : (h + 1) * shard], preferred_element_type=jnp.float32
            )
            .astype(jnp.bfloat16)
            .reshape(experts, 1, capacity, shard)
            for h in range(halves)
        ]
        moved = lax.all_to_all(
            jnp.concatenate(picked, axis=1), "expert", split_axis=0, concat_axis=0, tiled=True
        )
        return lax.all_to_all(
            moved.reshape(groups, capacity, shard), "dp", split_axis=0, concat_axis=0, tiled=True
        ).reshape(slots, shard)

    x_block = send(tokens)
    g_block = send(grad_out)
    gate = jnp.dot(x_block, gate_shard, preferred_element_type=jnp.float32)
    upper = jnp.dot(x_block, up_shard, preferred_element_type=jnp.float32)
    back = lax.dot_general(g_block, down_shard, last_dims, preferred_element_type=jnp.float32)
    mine = lax.psum_scatter(
        jnp.concatenate([gate, upper, back], axis=1).astype(jnp.bfloat16),
        "dp",
        scatter_dimension=0,
        tiled=True,
    ).astype(jnp.float32)
    gate = mine[:, :hidden]
    upper = mine[:, hidden : 2 * hidden]
    back = mine[:, 2 * hidden :] * own_weight[:, None]
    sigmoid_gate = jax.nn.sigmoid(gate)
    scaled = own_weight[:, None] * gate * sigmoid_gate * upper
    d_gate = back * upper * sigmoid_gate * (1.0 + gate * (1.0 - sigmoid_gate))
    d_up = back * gate * sigmoid_gate
    local = jnp.concatenate([scaled, d_gate, d_up], axis=1).astype(jnp.bfloat16)
    piece = lax.all_gather(local, "dp", axis=0, tiled=True)
    scaled = piece[:, :hidden]
    d_gate = piece[:, hidden : 2 * hidden]
    d_up = piece[:, 2 * hidden :]
    block_dx = lax.dot_general(
        d_gate, gate_shard, last_dims, preferred_element_type=jnp.float32
    ) + lax.dot_general(d_up, up_shard, last_dims, preferred_element_type=jnp.float32)
    dx_rows = block_dx.astype(jnp.bfloat16)
    returned = lax.all_to_all(
        dx_rows.reshape(groups, capacity, shard), "dp", split_axis=0, concat_axis=0, tiled=True
    )
    returned = lax.all_to_all(
        returned.reshape(experts, halves, capacity, shard),
        "expert",
        split_axis=0,
        concat_axis=0,
        tiled=True,
    )
    grad_g = lax.dot_general(x_block, d_gate, rows_first, preferred_element_type=jnp.float32)
    grad_u = lax.dot_general(x_block, d_up, rows_first, preferred_element_type=jnp.float32)
    grad_d = lax.dot_general(scaled, g_block, rows_first, preferred_element_type=jnp.float32)
    grad_tokens = jnp.concatenate(
        [
            lax.dot_general(
                dispatch,
                returned[:, h].reshape(experts * capacity, shard),
                rows_first,
                preferred_element_type=jnp.float32,
            ).astype(jnp.bfloat16)
            for h in range(halves)
        ],
        axis=1,
    )
    grad_gate = (grad_g * inv_root).astype(jnp.bfloat16)[None]
    grad_up = (grad_u * inv_root).astype(jnp.bfloat16)[None]
    grad_down = (grad_d * inv_root).astype(jnp.bfloat16)[None]
    return (grad_tokens, grad_gate, grad_up, grad_down)


def solution(mesh):
    in_specs = (
        P("dp", "expert"),
        P("dp", "expert"),
        P("dp", None),
        P("dp", None),
        P("expert", "dp", None),
        P("expert", "dp", None),
        P("expert", None, "dp"),
    )
    out_specs = (
        P("dp", "expert"),
        P("expert", "dp", None),
        P("expert", "dp", None),
        P("expert", None, "dp"),
    )
    return jax.shard_map(body, mesh=mesh, in_specs=in_specs, out_specs=out_specs, check_vma=False)
```

profile of v0, /device:TPU:1, one launch (start us, length us, event | category | flops | bytes accessed | tf_op | source)
XLA Modules:
  0.0 391.0 jit_solution(13324293775358559816)
XLA Ops:
  7.2 0.0 copy-start
  7.2 0.8 slice_bitcast_fusion.3
  8.0 0.1 eq.100
  8.1 0.1 fusion.34
  8.2 0.1 bitcast_compare_fusion
  8.4 1.2 convolution_convert_fusion.6
  9.6 1.3 convolution_convert_fusion.5
  10.9 0.2 copy.29
  11.1 0.2 copy.30
  11.4 0.0 copy-start.4
  11.4 0.1 pad_maximum_fusion.1
  11.5 1.1 copy.31
  12.6 6.4 %all-to-all-start = ((bf16[8,2,64,448]{3,2,1,0:T(8,128)(2,1)}), bf16[8,2,64,448]{3,2,1,0:T(8,128)(2,1)S(1)}, u32[]{:S(2)}, u32[]{:S(2)}) async-start(bf16[8,2,64,448]{3,2,1,0:T(8,128)(2,1)} %copy.31), calls=%async_computation | async-start | bytes 2097152 | tf_op jit(solution)/shard_map/all_to_all | solution.py:51
  18.9 0.0 copy-done.4
  18.9 1.1 convolution_convert_fusion.4
  20.0 1.2 copy.32
  21.3 2.1 convolution_convert_fusion.3
  23.3 2.0 copy.33
  25.4 1.2 pad_maximum_fusion.2
  26.5 1.1 copy.34
  27.6 7.2 %all-to-all-done = bf16[8,2,64,448]{3,2,1,0:T(8,128)(2,1)S(1)} async-done(((bf16[8,2,64,448]{3,2,1,0:T(8,128)(2,1)}), bf16[8,2,64,448]{3,2,1,0:T(8,128)(2,1)S(1)}, u32[]{:S(2)}, u32[]{:S(2)}) %all-to-all-start) | async-done | bytes 917536 | tf_op jit(solution)/shard_map/all_to_all | solution.py:51
  34.7 19.1 %all_to_all.30 = bf16[8,2,64,448]{3,2,1,0:T(8,128)(2,1)} all-to-all(bf16[8,2,64,448]{3,2,1,0:T(8,128)(2,1)} %copy.34), channel_id=1, replica_groups=mesh['expert'=8,'dp'=16] {'expert'}, dimensions={0} | all-to-all | bytes 1835008 | tf_op jit(solution)/shard_map/all_to_all | solution.py:51
  53.8 26.0 %all_to_all.31 = bf16[16,64,448]{2,1,0:T(8,128)(2,1)} all-to-all(bf16[16,64,448]{2,1,0:T(8,128)(2,1)S(1)} %bitcast.62), channel_id=1, replica_groups=mesh['expert'=8,'dp'=16] {'dp'}, dimensions={0} | all-to-all | bytes 1835008 | tf_op jit(solution)/shard_map/all_to_all | solution.py:54
  79.9 5.2 %all-to-all-start.3 = ((bf16[16,64,448]{2,1,0:T(8,128)(2,1)}), bf16[16,64,448]{2,1,0:T(8,128)(2,1)}, u32[]{:S(2)}, u32[]{:S(2)}) async-start(bf16[16,64,448]{2,1,0:T(8,128)(2,1)} %bitcast.63), calls=%async_computation.3 | async-start | bytes 2097152 | tf_op jit(solution)/shard_map/all_to_all | solution.py:54
  85.0 0.0 reduce-scatter.2.cloned.1.call-start
  85.1 0.0 copy-done
  85.1 0.0 copy-start.3
  85.1 0.0 copy-start.6
  85.1 5.7 %convolution_convert_fusion.1 = bf16[1024,2048]{1,0:T(8,128)(2,1)} fusion(bf16[1024,448]{1,0:T(8,128)(2,1)} %bitcast.70, bf16[1,448,2048]{2,1,0:T(8,128)(2,1)S(1)} %copy-done), kind=kOutput, calls=%fused_computation.4 | convolution fusion | flops 1881145344 | bytes 6946816 | tf_op jit(solution)/shard_map/dot_general | solution.py:61
  90.8 0.0 copy-done.3
  90.8 0.0 copy-done.6
  90.8 4.3 %convolution_convert_fusion.2 = bf16[1024,2048]{1,0:T(8,128)(2,1)} fusion(bf16[1024,448]{1,0:T(8,128)(2,1)S(1)} %bitcast.72, bf16[1,448,2048]{2,1,0:T(8,128)(2,1)S(1)} %copy-done.6), kind=kOutput, calls=%fused_computation.5 | convolution fusion | flops 1881145344 | bytes 6946816 | tf_op jit(solution)/shard_map/dot_general | solution.py:60
  95.1 7.5 %all-to-all-done.3 = bf16[16,64,448]{2,1,0:T(8,128)(2,1)} async-done(((bf16[16,64,448]{2,1,0:T(8,128)(2,1)}), bf16[16,64,448]{2,1,0:T(8,128)(2,1)}, u32[]{:S(2)}, u32[]{:S(2)}) %all-to-all-start.3) | async-done | bytes 917536 | tf_op jit(solution)/shard_map/all_to_all | solution.py:54
  102.6 0.0 copy-start.1
  102.6 0.0 copy-start.2
  102.6 4.3 %convolution_convert_fusion = bf16[1024,2048]{1,0:T(8,128)(2,1)S(1)} fusion(bf16[1024,448]{1,0:T(8,128)(2,1)} %bitcast.17, bf16[1,2048,448]{1,2,0:T(8,128)(2,1)} %param.13), kind=kOutput, calls=%fused_computation.3 | convolution fusion | flops 1881145344 | bytes 6946816 | tf_op jit(solution)/shard_map/dot_general | solution.py:62
  106.9 0.0 copy-done.1
  106.9 0.0 copy-done.2
  106.9 11.4 %pad_maximum_fusion = bf16[1024,6144]{1,0:T(8,128)(2,1)} fusion(bf16[1024,2048]{1,0:T(8,128)(2,1)S(1)} %convolution_convert_fusion, bf16[1024,2048]{1,0:T(8,128)(2,1)S(1)} %copy-done.1, bf16[1024,2048]{1,0:T(8,128)(2,1)S(1)} %copy-done.2), kind=kLoop, calls=%fused_computation | loop fusion | flops 37748736 | bytes 25165824 | tf_op jit(solution)/shard_map/concatenate | solution.py:64
  118.4 0.0 reduce-scatter.2.cloned.1.call-update
  118.4 0.2 all-gather.2.cloned.1.call-start
  118.6 0.4 copy-done.5
  119.1 0.1 select_reduce_fusion
  119.2 115.9 %reduce-scatter.2.cloned.1.call-done = bf16[64,6144]{1,0:T(8,128)(2,1)} async-done(((bf16[1024,6144]{1,0:T(8,128)(2,1)}), bf16[64,6144]{1,0:T(8,128)(2,1)}) %reduce-scatter.2.cloned.1.call-update) | async-done | bytes 786448 | tf_op jit(solution)/shard_map/reduce_scatter | solution.py:63
  235.0 1.2 convert_element_type.49
  236.3 0.4 multiply_convert_fusion.5
  236.7 0.9 pad_maximum_fusion.3
  237.6 0.0 all-gather.2.cloned.1.call-update
  237.6 91.2 %all-gather.2.cloned.1.call-done = bf16[1024,6144]{1,0:T(8,128)(2,1)} async-done(((bf16[64,6144]{1,0:T(8,128)(2,1)}), bf16[1024,6144]{1,0:T(8,128)(2,1)}) %all-gather.2.cloned.1.call-update) | async-done | bytes 12582928 | tf_op jit(solution)/shard_map/all_gather | solution.py:77
  328.8 4.4 %fusion.4 = f32[1024,448]{0,1:T(8,128)S(1)} fusion(bf16[1024,6144]{1,0:T(8,128)(2,1)} %all-gather.2.cloned.1.call-done, bf16[1,448,2048]{2,1,0:T(8,128)(2,1)S(1)} %copy-done), kind=kOutput, calls=%fused_computation.8 | convolution fusion | flops 1879048192 | bytes 7864320 | tf_op jit(solution)/shard_map/dot_general | solution.py:83
  333.2 0.0 copy-done.7
  333.2 5.3 %add_convert_fusion = bf16[1024,448]{0,1:T(8,128)(2,1)} fusion(f32[1024,448]{0,1:T(8,128)S(1)} %fusion.4, bf16[1,448,2048]{2,1,0:T(8,128)(2,1)S(1)} %copy-done.7, bf16[1024,6144]{1,0:T(8,128)(2,1)} %all-gather.2.cloned.1.call-done), kind=kOutput, calls=%fused_computation.25 | convolution fusion | flops 1879965696 | bytes 8781824 | tf_op jit(solution)/shard_map/dot_general | solution.py:81
  338.5 2.2 copy.35
  340.8 4.3 %all-to-all-start.4 = ((bf16[16,64,448]{2,1,0:T(8,128)(2,1)}), bf16[16,64,448]{2,1,0:T(8,128)(2,1)}, u32[]{:S(2)}, u32[]{:S(2)}) async-start(bf16[16,64,448]{2,1,0:T(8,128)(2,1)} %bitcast.19), calls=%async_computation.5 | async-start | bytes 2097152 | tf_op jit(solution)/shard_map/all_to_all | solution.py:85
  345.1 5.5 %fusion.16 = bf16[1,448,2048]{2,1,0:T(8,128)(2,1)} fusion(bf16[1024,448]{1,0:T(8,128)(2,1)S(1)} %bitcast.73, bf16[1024,6144]{1,0:T(8,128)(2,1)} %all-gather.2.cloned.1.call-done), kind=kOutput, calls=%fused_computation.17 | convolution fusion | flops 1880883200 | bytes 6946816 | tf_op jit(solution)/shard_map/dot_general | solution.py:95
  350.6 12.0 %all-to-all-done.4 = bf16[16,64,448]{2,1,0:T(8,128)(2,1)} async-done(((bf16[16,64,448]{2,1,0:T(8,128)(2,1)}), bf16[16,64,448]{2,1,0:T(8,128)(2,1)}, u32[]{:S(2)}, u32[]{:S(2)}) %all-to-all-start.4) | async-done | bytes 917536 | tf_op jit(solution)/shard_map/all_to_all | solution.py:85
  362.7 4.1 %all-to-all-start.5 = ((bf16[8,2,64,448]{3,2,1,0:T(8,128)(2,1)}), bf16[8,2,64,448]{3,2,1,0:T(8,128)(2,1)S(1)}, u32[]{:S(2)}, u32[]{:S(2)}) async-start(bf16[8,2,64,448]{3,2,1,0:T(8,128)(2,1)} %bitcast.20), calls=%async_computation.6 | async-start | bytes 2097152 | tf_op jit(solution)/shard_map/all_to_all | solution.py:88
  366.8 5.8 %fusion.19 = bf16[1,448,2048]{2,1,0:T(8,128)(2,1)} fusion(bf16[1024,448]{1,0:T(8,128)(2,1)} %bitcast.71, bf16[1024,6144]{1,0:T(8,128)(2,1)} %all-gather.2.cloned.1.call-done), kind=kOutput, calls=%fused_computation.18 | convolution fusion | flops 1880883200 | bytes 7077888 | tf_op jit(solution)/shard_map/dot_general | solution.py:96
  372.6 5.9 %fusion.22 = bf16[1,2048,448]{1,2,0:T(8,128)(2,1)} fusion(bf16[1024,448]{1,0:T(8,128)(2,1)} %bitcast.17, bf16[1024,6144]{1,0:T(8,128)(2,1)} %all-gather.2.cloned.1.call-done), kind=kOutput, calls=%fused_computation.19 | convolution fusion | flops 1880883200 | bytes 7077888 | tf_op jit(solution)/shard_map/dot_general | solution.py:97
  378.4 4.1 %all-to-all-done.5 = bf16[8,2,64,448]{3,2,1,0:T(8,128)(2,1)S(1)} async-done(((bf16[8,2,64,448]{3,2,1,0:T(8,128)(2,1)}), bf16[8,2,64,448]{3,2,1,0:T(8,128)(2,1)S(1)}, u32[]{:S(2)}, u32[]{:S(2)}) %all-to-all-start.5) | async-done | bytes 917536 | tf_op jit(solution)/shard_map/all_to_all | solution.py:88
  382.6 0.1 fusion.44
  382.7 0.3 convolution_convert_fusion.8
  383.0 0.3 convolution_convert_fusion.7
  383.4 0.8 copy.36
  (9 shorter events, 0.1 us)
Async XLA Ops:
  7.2 77.9 %copy-start = (bf16[1,448,2048]{2,1,0:T(8,128)(2,1)S(1)}, bf16[1,448,2048]{2,1,0:T(8,128)(2,1)}, u32[]{:S(2)}) copy-start(bf16[1,448,2048]{2,1,0:T(8,128)(2,1)} %param.12) | copy-start | bytes 5505028
  11.4 7.6 %copy-start.4 = (bf16[128,896]{1,0:T(8,128)(2,1)S(1)}, bf16[128,896]{1,0:T(8,128)(2,1)}, u32[]{:S(2)}) copy-start(bf16[128,896]{1,0:T(8,128)(2,1)} %param.8) | copy-start | bytes 688132
  12.6 22.2 %all-to-all-start = ((bf16[8,2,64,448]{3,2,1,0:T(8,128)(2,1)}), bf16[8,2,64,448]{3,2,1,0:T(8,128)(2,1)S(1)}, u32[]{:S(2)}, u32[]{:S(2)}) async-start(bf16[8,2,64,448]{3,2,1,0:T(8,128)(2,1)} %copy.31), calls=%async_computation | async-start | bytes 2097152 | tf_op jit(solution)/shard_map/all_to_all | solution.py:51
  79.9 22.7 %all-to-all-start.3 = ((bf16[16,64,448]{2,1,0:T(8,128)(2,1)}), bf16[16,64,448]{2,1,0:T(8,128)(2,1)}, u32[]{:S(2)}, u32[]{:S(2)}) async-start(bf16[16,64,448]{2,1,0:T(8,128)(2,1)} %bitcast.63), calls=%async_computation.3 | async-start | bytes 2097152 | tf_op jit(solution)/shard_map/all_to_all | solution.py:54
  85.0 150.0 %reduce-scatter.2.cloned.1.call-start = ((), (), s32[]{:S(2)}) async-start(), calls=%async_computation.7 | async-start | bytes 13369344 | tf_op jit(solution)/shard_map/reduce_scatter | solution.py:63
  85.1 5.7 %copy-start.3 = (bf16[16,64,448]{2,1,0:T(8,128)(2,1)S(1)}, bf16[16,64,448]{2,1,0:T(8,128)(2,1)}, u32[]{:S(2)}) copy-start(bf16[16,64,448]{2,1,0:T(8,128)(2,1)} %all_to_all.31) | copy-start | bytes 2752516
  85.1 5.7 %copy-start.6 = (bf16[1,448,2048]{2,1,0:T(8,128)(2,1)S(1)}, bf16[1,448,2048]{2,1,0:T(8,128)(2,1)}, u32[]{:S(2)}) copy-start(bf16[1,448,2048]{2,1,0:T(8,128)(2,1)} %param.11) | copy-start | bytes 5505028
  102.6 4.3 %copy-start.1 = (bf16[1024,2048]{1,0:T(8,128)(2,1)S(1)}, bf16[1024,2048]{1,0:T(8,128)(2,1)}, u32[]{:S(2)}) copy-start(bf16[1024,2048]{1,0:T(8,128)(2,1)} %convolution_convert_fusion.1) | copy-start | bytes 12582916
  102.6 4.3 %copy-start.2 = (bf16[1024,2048]{1,0:T(8,128)(2,1)S(1)}, bf16[1024,2048]{1,0:T(8,128)(2,1)}, u32[]{:S(2)}) copy-start(bf16[1024,2048]{1,0:T(8,128)(2,1)} %convolution_convert_fusion.2) | copy-start | bytes 12582916
  118.4 0.7 copy-start.5
  118.4 210.4 %all-gather.2.cloned.1.call-start = ((), (), s32[]{:S(2)}) async-start(), calls=%async_computation.8 | async-start | bytes 13369344 | tf_op jit(solution)/shard_map/all_gather | solution.py:77
  328.8 4.4 %copy-start.7 = (bf16[1,448,2048]{2,1,0:T(8,128)(2,1)S(1)}, bf16[1,448,2048]{2,1,0:T(8,128)(2,1)}, u32[]{:S(2)}) copy-start(bf16[1,448,2048]{2,1,0:T(8,128)(2,1)} %param.11) | copy-start | bytes 5505028
  340.8 21.9 %all-to-all-start.4 = ((bf16[16,64,448]{2,1,0:T(8,128)(2,1)}), bf16[16,64,448]{2,1,0:T(8,128)(2,1)}, u32[]{:S(2)}, u32[]{:S(2)}) async-start(bf16[16,64,448]{2,1,0:T(8,128)(2,1)} %bitcast.19), calls=%async_computation.5 | async-start | bytes 2097152 | tf_op jit(solution)/shard_map/all_to_all | solution.py:85
  362.7 19.9 %all-to-all-start.5 = ((bf16[8,2,64,448]{3,2,1,0:T(8,128)(2,1)}), bf16[8,2,64,448]{3,2,1,0:T(8,128)(2,1)S(1)}, u32[]{:S(2)}, u32[]{:S(2)}) async-start(bf16[8,2,64,448]{3,2,1,0:T(8,128)(2,1)} %bitcast.20), calls=%async_computation.6 | async-start | bytes 2097152 | tf_op jit(solution)/shard_map/all_to_all | solution.py:88
Sparse Core Ops, SparseCore 0:
  118.5 116.5 reduce-scatter.1
  238.4 90.3 all-gather.1
where the time goes:
time: 392 us; the launch traced here: 391 us
  waiting for transfers between devices  238 us (61%)
  matrix products  47.8 us (12%)
  blocking collectives  45.1 us (12%)
  starting transfers between devices  20.2 us (5%)
  other arithmetic  15.6 us (4%)
  between operations  14.2 us (4%)
  local copies, waits for them, and re-layouts  10.3 us (3%)
    reduce_scatter x1, waiting for transfers between devices, body(): lax.psum_scatter(jnp.concatenate([gate, upper, back], axis=1).astype(jnp....  116 us
    all_gather x1, waiting for transfers between devices, body(): piece = lax.all_gather(local, 'dp', axis=0, tiled=True)  91.2 us
    all_to_all x1, blocking collectives, send(): lax.all_to_all(moved.reshape(groups, capacity, shard), 'dp', split_axis=0...  26 us
    all_to_all x1, blocking collectives, send(): lax.all_to_all(jnp.concatenate(picked, axis=1), 'expert', split_axis=0, c...  19.1 us
    all_to_all x1, waiting for transfers between devices, body(): lax.all_to_all(dx_rows.reshape(groups, capacity, shard), 'dp', split_axis...  12 us
    concatenate x1, other arithmetic, body(): jnp.concatenate([gate, upper, back], axis=1).astype(jnp.bfloat16)  11.4 us
  transfers between devices with their start and end apart: 6, of which 6 were waited for; matrix products, arithmetic and copies ran while one was open for 9% of the time, Pallas kernels for 0%

commit v1 on v0

--- a/solution.py
+++ b/solution.py
@@ -74,7 +74,9 @@
     d_gate = back * upper * sigmoid_gate * (1.0 + gate * (1.0 - sigmoid_gate))
     d_up = back * gate * sigmoid_gate
     local = jnp.concatenate([scaled, d_gate, d_up], axis=1).astype(jnp.bfloat16)
-    piece = lax.all_gather(local, "dp", axis=0, tiled=True)
+    piece = jnp.concatenate(
+        lax.all_to_all(jnp.stack([local] * lax.axis_size("dp")), "dp", 0, 0), axis=0
+    )
     scaled = piece[:, :hidden]
     d_gate = piece[:, hidden : 2 * hidden]
     d_up = piece[:, 2 * hidden :]

time: 392 us -> 450 us (1.15)
  blocking collectives: 45.1 us -> 191 us
  waiting for transfers between devices: 238 us -> 147 us
  local copies, waits for them, and re-layouts: 10.3 us -> 19.5 us
  matrix products: 47.8 us -> 42.9 us
    all_to_all x0 -> x1, blocking collectives: none -> 146 us  [body(): lax.all_to_all(jnp.stack([local] * lax.axis_size('dp')), 'dp', 0, 0)]
    all_gather x1 -> x0, waiting for transfers between devices: 91.2 us -> none  [body(): piece = lax.all_gather(local, 'dp', axis=0, tiled=True)]
    another operation x0 -> x1, local copies, waits for them, and re-layouts: none -> 6.11 us  [body(): jnp.stack([local] * lax.axis_size('dp'))]
  transfers between devices with their start and end apart: 6 -> 5, of which waited for: 6 -> 5; matrix products, arithmetic and copies ran while one was open for 9% -> 8% of each run, Pallas kernels for 0% -> 0%
where the time goes in v1:
time: 450 us; the launch traced here: 449 us
  blocking collectives  191 us (42%)
  waiting for transfers between devices  147 us (33%)
  matrix products  42.9 us (10%)
  starting transfers between devices  20.6 us (5%)
  local copies, waits for them, and re-layouts  19.5 us (4%)
  other arithmetic  14.5 us (3%)
  between operations  14.3 us (3%)
    all_to_all x1, blocking collectives, body(): lax.all_to_all(jnp.stack([local] * lax.axis_size('dp')), 'dp', 0, 0)  146 us
    reduce_scatter x1, waiting for transfers between devices, body(): lax.psum_scatter(jnp.concatenate([gate, upper, back], axis=1).astype(jnp....  116 us
    all_to_all x1, blocking collectives, send(): lax.all_to_all(moved.reshape(groups, capacity, shard), 'dp', split_axis=0...  26 us
    all_to_all x1, blocking collectives, send(): lax.all_to_all(jnp.concatenate(picked, axis=1), 'expert', split_axis=0, c...  19.1 us
    all_to_all x1, waiting for transfers between devices, body(): lax.all_to_all(dx_rows.reshape(groups, capacity, shard), 'dp', split_axis...  12 us
    concatenate x1, other arithmetic, body(): jnp.concatenate([gate, upper, back], axis=1).astype(jnp.bfloat16)  11.3 us
  transfers between devices with their start and end apart: 5, of which 5 were waited for; matrix products, arithmetic and copies ran while one was open for 8% of the time, Pallas kernels for 0%

profile of v1, /device:TPU:1, one launch (start us, length us, event | category | flops | bytes accessed | tf_op | source)
XLA Modules:
  0.0 449.3 jit_solution(7191823632857937329)
XLA Ops:
  7.2 0.0 copy-start
  7.2 0.8 slice_bitcast_fusion.3
  8.0 0.1 eq.100
  8.1 0.1 fusion.34
  8.2 0.1 bitcast_compare_fusion
  8.4 1.2 convolution_convert_fusion.6
  9.6 1.3 convolution_convert_fusion.5
  10.9 0.2 copy.29
  11.1 0.2 copy.30
  11.4 0.0 copy-start.8
  11.4 0.1 pad_maximum_fusion.1
  11.5 1.1 copy.31
  12.6 6.4 %all-to-all-start = ((bf16[8,2,64,448]{3,2,1,0:T(8,128)(2,1)}), bf16[8,2,64,448]{3,2,1,0:T(8,128)(2,1)S(1)}, u32[]{:S(2)}, u32[]{:S(2)}) async-start(bf16[8,2,64,448]{3,2,1,0:T(8,128)(2,1)} %copy.31), calls=%async_computation | async-start | bytes 2097152 | tf_op jit(solution)/shard_map/all_to_all | solution.py:51
  18.9 0.0 copy-done.8
  18.9 1.1 convolution_convert_fusion.4
  20.0 1.2 copy.32
  21.3 2.1 convolution_convert_fusion.3
  23.3 2.0 copy.33
  25.4 1.2 pad_maximum_fusion.2
  26.5 1.1 copy.34
  27.6 7.2 %all-to-all-done = bf16[8,2,64,448]{3,2,1,0:T(8,128)(2,1)S(1)} async-done(((bf16[8,2,64,448]{3,2,1,0:T(8,128)(2,1)}), bf16[8,2,64,448]{3,2,1,0:T(8,128)(2,1)S(1)}, u32[]{:S(2)}, u32[]{:S(2)}) %all-to-all-start) | async-done | bytes 917536 | tf_op jit(solution)/shard_map/all_to_all | solution.py:51
  34.7 19.1 %all_to_all.35 = bf16[8,2,64,448]{3,2,1,0:T(8,128)(2,1)} all-to-all(bf16[8,2,64,448]{3,2,1,0:T(8,128)(2,1)} %copy.34), channel_id=1, replica_groups=mesh['expert'=8,'dp'=16] {'expert'}, dimensions={0} | all-to-all | bytes 1835008 | tf_op jit(solution)/shard_map/all_to_all | solution.py:51
  53.8 26.0 %all_to_all.36 = bf16[16,64,448]{2,1,0:T(8,128)(2,1)} all-to-all(bf16[16,64,448]{2,1,0:T(8,128)(2,1)S(1)} %bitcast.68), channel_id=1, replica_groups=mesh['expert'=8,'dp'=16] {'dp'}, dimensions={0} | all-to-all | bytes 1835008 | tf_op jit(solution)/shard_map/all_to_all | solution.py:54
  79.9 4.5 %all-to-all-start.3 = ((bf16[16,64,448]{2,1,0:T(8,128)(2,1)}), bf16[16,64,448]{2,1,0:T(8,128)(2,1)S(1)}, u32[]{:S(2)}, u32[]{:S(2)}) async-start(bf16[16,64,448]{2,1,0:T(8,128)(2,1)} %bitcast.69), calls=%async_computation.3 | async-start | bytes 2097152 | tf_op jit(solution)/shard_map/all_to_all | solution.py:54
  84.4 0.2 reduce-scatter.2.cloned.1.call-start
  84.6 0.0 copy-done
  84.6 0.0 copy-start.4
  84.6 0.0 copy-start.10
  84.6 5.7 %convolution_convert_fusion.1 = bf16[1024,2048]{1,0:T(8,128)(2,1)} fusion(bf16[1024,448]{1,0:T(8,128)(2,1)} %bitcast.76, bf16[1,448,2048]{2,1,0:T(8,128)(2,1)S(1)} %copy-done), kind=kOutput, calls=%fused_computation.4 | convolution fusion | flops 1881145344 | bytes 6946816 | tf_op jit(solution)/shard_map/dot_general | solution.py:61
  90.3 0.0 copy-done.4
  90.3 0.0 copy-done.10
  90.3 4.3 convolution_convert_fusion.2
  94.6 7.2 %all-to-all-done.3 = bf16[16,64,448]{2,1,0:T(8,128)(2,1)S(1)} async-done(((bf16[16,64,448]{2,1,0:T(8,128)(2,1)}), bf16[16,64,448]{2,1,0:T(8,128)(2,1)S(1)}, u32[]{:S(2)}, u32[]{:S(2)}) %all-to-all-start.3) | async-done | bytes 917536 | tf_op jit(solution)/shard_map/all_to_all | solution.py:54
  101.8 4.3 convolution_convert_fusion
  106.1 0.0 copy-done.6
  106.1 0.1 copy-done.3
  106.2 11.3 %pad_maximum_fusion = bf16[1024,6144]{1,0:T(8,128)(2,1)} fusion(bf16[1024,2048]{1,0:T(8,128)(2,1)S(1)} %convolution_convert_fusion, bf16[1024,2048]{1,0:T(8,128)(2,1)S(1)} %copy-done.2, bf16[1024,2048]{1,0:T(8,128)(2,1)S(1)} %copy-done.3), kind=kLoop, calls=%fused_computation | loop fusion | flops 37748736 | bytes 25165824 | tf_op jit(solution)/shard_map/concatenate | solution.py:64
  117.5 0.0 reduce-scatter.2.cloned.1.call-update
  117.5 0.6 copy-done.9
  118.2 0.1 select_reduce_fusion
  118.3 115.9 %reduce-scatter.2.cloned.1.call-done = bf16[64,6144]{1,0:T(8,128)(2,1)} async-done(((bf16[1024,6144]{1,0:T(8,128)(2,1)}), bf16[64,6144]{1,0:T(8,128)(2,1)}) %reduce-scatter.2.cloned.1.call-update) | async-done | bytes 786448 | tf_op jit(solution)/shard_map/reduce_scatter | solution.py:63
  234.2 1.2 convert_element_type.51
  235.4 0.4 multiply_convert_fusion.5
  235.8 0.1 pad_maximum_fusion.3
  235.9 6.1 %stack.2 = bf16[16,64,6144]{2,1,0:T(8,128)(2,1)} broadcast(bf16[64,6144]{1,0:T(8,128)(2,1)S(1)} %pad_maximum_fusion.3), dimensions={1,2} | broadcast | bytes 13369344 | tf_op jit(solution)/shard_map/stack | solution.py:78
  242.0 145.8 %all_to_all.37 = bf16[16,64,6144]{2,1,0:T(8,128)(2,1)S(1)} all-to-all(bf16[16,64,6144]{2,1,0:T(8,128)(2,1)} %stack.2), channel_id=1, replica_groups=mesh['expert'=8,'dp'=16] {'dp'}, dimensions={0} | all-to-all | bytes 25165824 | tf_op jit(solution)/shard_map/all_to_all | solution.py:78
  387.7 2.1 fusion.4
  389.8 2.7 copy-done.1
  392.5 0.0 copy-done.11
  392.5 3.0 add_convert_fusion
  395.6 2.3 copy.35
  397.9 5.1 %all-to-all-start.5 = ((bf16[16,64,448]{2,1,0:T(8,128)(2,1)}), bf16[16,64,448]{2,1,0:T(8,128)(2,1)}, u32[]{:S(2)}, u32[]{:S(2)}) async-start(bf16[16,64,448]{2,1,0:T(8,128)(2,1)} %bitcast.20), calls=%async_computation.6 | async-start | bytes 2097152 | tf_op jit(solution)/shard_map/all_to_all | solution.py:87
  403.1 0.0 copy-done.5
  403.1 5.5 %fusion.16 = bf16[1,448,2048]{2,1,0:T(8,128)(2,1)} fusion(bf16[1024,448]{1,0:T(8,128)(2,1)S(1)} %bitcast.79, bf16[1024,6144]{1,0:T(8,128)(2,1)} %bitcast.65), kind=kOutput, calls=%fused_computation.17 | convolution fusion | flops 1880883200 | bytes 6946816 | tf_op jit(solution)/shard_map/dot_general | solution.py:97
  408.6 12.0 %all-to-all-done.5 = bf16[16,64,448]{2,1,0:T(8,128)(2,1)} async-done(((bf16[16,64,448]{2,1,0:T(8,128)(2,1)}), bf16[16,64,448]{2,1,0:T(8,128)(2,1)}, u32[]{:S(2)}, u32[]{:S(2)}) %all-to-all-start.5) | async-done | bytes 917536 | tf_op jit(solution)/shard_map/all_to_all | solution.py:87
  420.6 4.4 all-to-all-start.6
  425.0 5.9 %fusion.19 = bf16[1,448,2048]{2,1,0:T(8,128)(2,1)} fusion(bf16[1024,448]{1,0:T(8,128)(2,1)} %bitcast.77, bf16[1024,6144]{1,0:T(8,128)(2,1)} %bitcast.66), kind=kOutput, calls=%fused_computation.18 | convolution fusion | flops 1880883200 | bytes 7077888 | tf_op jit(solution)/shard_map/dot_general | solution.py:98
  430.9 0.0 copy-done.7
  430.9 5.5 %fusion.22 = bf16[1,2048,448]{1,2,0:T(8,128)(2,1)} fusion(bf16[1024,448]{1,0:T(8,128)(2,1)S(1)} %bitcast.81, bf16[1024,6144]{1,0:T(8,128)(2,1)} %bitcast.67), kind=kOutput, calls=%fused_computation.19 | convolution fusion | flops 1880883200 | bytes 6946816 | tf_op jit(solution)/shard_map/dot_general | solution.py:99
  436.5 4.3 all-to-all-done.6
  440.8 0.1 fusion.44
  440.9 0.3 convolution_convert_fusion.8
  441.3 0.3 convolution_convert_fusion.7
  441.6 0.8 copy.36
  (16 shorter events, 0.1 us)
Async XLA Ops:
  7.2 77.4 %copy-start = (bf16[1,448,2048]{2,1,0:T(8,128)(2,1)S(1)}, bf16[1,448,2048]{2,1,0:T(8,128)(2,1)}, u32[]{:S(2)}) copy-start(bf16[1,448,2048]{2,1,0:T(8,128)(2,1)} %param.12) | copy-start | bytes 5505028
  11.4 7.6 %copy-start.8 = (bf16[128,896]{1,0:T(8,128)(2,1)S(1)}, bf16[128,896]{1,0:T(8,128)(2,1)}, u32[]{:S(2)}) copy-start(bf16[128,896]{1,0:T(8,128)(2,1)} %param.8) | copy-start | bytes 688132
  12.6 22.2 %all-to-all-start = ((bf16[8,2,64,448]{3,2,1,0:T(8,128)(2,1)}), bf16[8,2,64,448]{3,2,1,0:T(8,128)(2,1)S(1)}, u32[]{:S(2)}, u32[]{:S(2)}) async-start(bf16[8,2,64,448]{3,2,1,0:T(8,128)(2,1)} %copy.31), calls=%async_computation | async-start | bytes 2097152 | tf_op jit(solution)/shard_map/all_to_all | solution.py:51
  79.9 22.0 %all-to-all-start.3 = ((bf16[16,64,448]{2,1,0:T(8,128)(2,1)}), bf16[16,64,448]{2,1,0:T(8,128)(2,1)S(1)}, u32[]{:S(2)}, u32[]{:S(2)}) async-start(bf16[16,64,448]{2,1,0:T(8,128)(2,1)} %bitcast.69), calls=%async_computation.3 | async-start | bytes 2097152 | tf_op jit(solution)/shard_map/all_to_all | solution.py:54
  84.4 149.8 %reduce-scatter.2.cloned.1.call-start = ((), (), s32[]{:S(2)}) async-start(), calls=%async_computation.8 | async-start | bytes 13369344 | tf_op jit(solution)/shard_map/reduce_scatter | solution.py:63
  84.6 5.7 %copy-start.4 = (bf16[16,64,448]{2,1,0:T(8,128)(2,1)S(1)}, bf16[16,64,448]{2,1,0:T(8,128)(2,1)}, u32[]{:S(2)}) copy-start(bf16[16,64,448]{2,1,0:T(8,128)(2,1)} %all_to_all.36) | copy-start | bytes 2752516
  84.6 5.7 %copy-start.10 = (bf16[1,448,2048]{2,1,0:T(8,128)(2,1)S(1)}, bf16[1,448,2048]{2,1,0:T(8,128)(2,1)}, u32[]{:S(2)}) copy-start(bf16[1,448,2048]{2,1,0:T(8,128)(2,1)} %param.11) | copy-start | bytes 5505028
  101.8 4.3 copy-start.6
  101.8 4.3 copy-start.2
  101.8 4.4 copy-start.3
  117.5 0.7 copy-start.9
  387.7 4.8 %copy-start.1 = (bf16[16,64,6144]{2,1,0:T(8,128)(2,1)}, bf16[16,64,6144]{2,1,0:T(8,128)(2,1)S(1)}, u32[]{:S(2)}) copy-start(bf16[16,64,6144]{2,1,0:T(8,128)(2,1)S(1)} %all_to_all.37) | copy-start | bytes 37748740
  387.7 4.8 %copy-start.11 = (bf16[1,448,2048]{2,1,0:T(8,128)(2,1)S(1)}, bf16[1,448,2048]{2,1,0:T(8,128)(2,1)}, u32[]{:S(2)}) copy-start(bf16[1,448,2048]{2,1,0:T(8,128)(2,1)} %param.11) | copy-start | bytes 5505028
  395.6 7.5 %copy-start.5 = (bf16[16,64,448]{2,1,0:T(8,128)(2,1)S(1)}, bf16[16,64,448]{2,1,0:T(8,128)(2,1)}, u32[]{:S(2)}) copy-start(bf16[16,64,448]{2,1,0:T(8,128)(2,1)} %all_to_all.36) | copy-start | bytes 2752516
  397.9 22.7 %all-to-all-start.5 = ((bf16[16,64,448]{2,1,0:T(8,128)(2,1)}), bf16[16,64,448]{2,1,0:T(8,128)(2,1)}, u32[]{:S(2)}, u32[]{:S(2)}) async-start(bf16[16,64,448]{2,1,0:T(8,128)(2,1)} %bitcast.20), calls=%async_computation.6 | async-start | bytes 2097152 | tf_op jit(solution)/shard_map/all_to_all | solution.py:87
  420.6 20.2 %all-to-all-start.6 = ((bf16[8,2,64,448]{3,2,1,0:T(8,128)(2,1)}), bf16[8,2,64,448]{3,2,1,0:T(8,128)(2,1)S(1)}, u32[]{:S(2)}, u32[]{:S(2)}) async-start(bf16[8,2,64,448]{3,2,1,0:T(8,128)(2,1)} %bitcast.21), calls=%async_computation.7 | async-start | bytes 2097152 | tf_op jit(solution)/shard_map/all_to_all | solution.py:90
  425.0 5.9 %copy-start.7 = (bf16[16,64,448]{2,1,0:T(8,128)(2,1)S(1)}, bf16[16,64,448]{2,1,0:T(8,128)(2,1)}, u32[]{:S(2)}) copy-start(bf16[16,64,448]{2,1,0:T(8,128)(2,1)} %copy-done.6) | copy-start | bytes 2752516
Sparse Core Ops, SparseCore 0:
  117.6 116.5 reduce-scatter.1
